TPU v7x, 512 devices: a whole 4x8x8 slice. The times are simulated.
512 devices in a mesh: tok: 128 (over z, y, core), head: 4 (over x).
Axes of the slice: x: 4, y: 8, z: 8, core: 2. Of those that a mesh axis runs over, the one named last changes fastest.
Arguments:
- query_rows: bfloat16 [24576, 1536], P('tok', 'head'), may hold values from -5 to 5
- key_rows: bfloat16 [24576, 1536], P('tok', 'head'), may hold values from -5 to 5
- value_rows: bfloat16 [24576, 1536], P('tok', 'head'), may hold values from -8 to 8
- neighbours: int32 [128, 27], replicated, may hold values from -1 to 127, as said below
- out_weight: bfloat16 [1536, 3072], P('head'), may hold values from -0.15625 to 0.15625
- out_grad: bfloat16 [24576, 3072], P(('tok', 'head')), may hold values from -6 to 6
Outputs:
- attended: bfloat16 [24576, 1536], P('tok', 'head')
- grad_queries: bfloat16 [24576, 1536], P('tok', 'head')
- grad_keys: bfloat16 [24576, 1536], P('tok', 'head')
- grad_values: bfloat16 [24576, 1536], P('tok', 'head')
Inputs may be any that keep to these rules, and one draw needn't show every extreme that they name: `neighbours`: tile t lies at time tile t % 1 of device block b = t, and block b at tile row b // 8 and tile column b % 8 of a grid of 16 x 8 blocks. Entry (a + 1) * 9 + (b + 1) * 3 + (c + 1) of a tile's list, for a, b, c in -1, 0, 1, is either -1 or the tile displaced by a time tiles, b tile rows and c tile columns inside the grid; entry 13 is the tile itself; the listed tiles form a box around it.
All inputs are finite; a program needn't handle non-finite values.
Results may differ from a plain program's by a relative error of at most 0.02.
Values may be sent and summed in bfloat16 or wider, within the bound.
A program may use at most 64 MiB of HBM per device.

v0:
```python
import math

import jax
import jax.numpy as jnp
from jax import lax
from jax.sharding import PartitionSpec as P

HEAD_DIM = 128
TIME_TILES = 1
GRID_W = 8


def as_sent(array):
    return jax.tree.map(lambda a: a.astype(jnp.bfloat16) if a.dtype == jnp.float32 else a, array)


def shifted(value, axis, steps):
    count = lax.axis_size(axis)
    first, last = (max(0, -steps), min(count, count - steps))
    return lax.ppermute(value, axis, [(source, source + steps) for source in range(first, last)])


def stack_tree(collected):
    return jax.tree.map(lambda *leaves: jnp.stack(leaves), *collected)


def offset_of(offset_slot, grid_width):
    return (offset_slot // 3 - 1) * grid_width + (offset_slot % 3 - 1)


def fetch_each(pieces, shifter, grid_width):
    collected = []
    for offset_slot in range(9):
        offset = offset_of(offset_slot, grid_width)
        if offset == 0:
            collected.append(pieces)
        else:
            collected.append(shifter(pieces, -offset))
    return stack_tree(collected)


def return_each(partials, shifter, grid_width):
    summed = jax.tree.map(lambda leaf_array: leaf_array[4].astype(jnp.float32), partials)
    for offset_slot in range(9):
        offset = offset_of(offset_slot, grid_width)
        if offset != 0:
            one_piece = jax.tree.map(lambda leaf_array: leaf_array[offset_slot], partials)
            arrived = shifter(one_piece, offset)
            summed = jax.tree.map(
                lambda total_leaf, new_leaf: total_leaf + new_leaf.astype(jnp.float32),
                summed,
                arrived,
            )
    return summed


def forward_allowed(own_lists, time_tiles):
    query_time = jnp.arange(time_tiles)[:, None, None]
    offset_slot = jnp.arange(9)[None, :, None]
    key_time = jnp.arange(time_tiles)[None, None, :]
    time_step = key_time - query_time
    slot_index = jnp.clip((time_step + 1) * 9 + offset_slot, 0, 26)
    listed = own_lists[query_time, slot_index]
    return (jnp.abs(time_step) <= 1) & (listed >= 0)


def contract_last(left_matrix, right_matrix):
    return lax.dot_general(
        left_matrix, right_matrix, (((1,), (1,)), ((), ())), preferred_element_type=jnp.float32
    )


def contract_first(left_matrix, right_matrix):
    return lax.dot_general(
        left_matrix, right_matrix, (((0,), (0,)), ((), ())), preferred_element_type=jnp.float32
    )


def local(query_rows, key_rows, value_rows, neighbours, out_weight, out_grad):
    row_count, column_count = query_rows.shape
    head_count = column_count // HEAD_DIM
    tile_rows = row_count // TIME_TILES
    score_scale = 1.0 / math.sqrt(HEAD_DIM)
    position = lax.axis_index("tok")
    own_lists = lax.dynamic_slice_in_dim(neighbours, position * TIME_TILES, TIME_TILES, 0)

    def shift_keys(pieces, distance):
        return jax.tree.map(
            lambda part, own: part.astype(own.dtype),
            shifted(as_sent(pieces), "tok", distance),
            pieces,
        )

    near_keys, near_values = fetch_each((key_rows, value_rows), shift_keys, GRID_W)
    key_flat = near_keys.reshape(9 * row_count, column_count)
    value_flat = near_values.reshape(9 * row_count, column_count)
    allowed = forward_allowed(own_lists, TIME_TILES)[:, None, :, :, None]
    block_shape = (TIME_TILES, tile_rows, 9, TIME_TILES, tile_rows)
    weights_list = []
    logsum_list = []
    attended_list = []
    for head_index in range(head_count):
        columns = slice(head_index * HEAD_DIM, (head_index + 1) * HEAD_DIM)
        scores = contract_last(query_rows[:, columns], key_flat[:, columns]) * score_scale
        scores = jnp.where(allowed, scores.reshape(block_shape), -jnp.inf).reshape(
            row_count, 9 * row_count
        )
        row_max = jnp.max(scores, axis=1, keepdims=True)
        logsum = row_max + jnp.log(jnp.sum(jnp.exp(scores - row_max), axis=1, keepdims=True))
        weights = jnp.exp(scores - logsum).astype(jnp.bfloat16)
        attended_list.append(
            jnp.dot(weights, value_flat[:, columns], preferred_element_type=jnp.float32).astype(
                jnp.bfloat16
            )
        )
        weights_list.append(weights)
        logsum_list.append(logsum[:, 0])
    attended = jnp.concatenate(attended_list, 1)
    whole_grad = lax.all_gather(out_grad, "head", axis=0, tiled=True)
    attended_grad = contract_last(whole_grad, out_weight).astype(jnp.bfloat16)
    delta_list = []
    for head_index in range(head_count):
        columns = slice(head_index * HEAD_DIM, (head_index + 1) * HEAD_DIM)
        delta_list.append(
            jnp.sum(
                attended_grad[:, columns].astype(jnp.float32)
                * attended[:, columns].astype(jnp.float32),
                axis=1,
            )
        )
    query_grads = []
    key_parts = []
    value_parts = []
    for head_index in range(head_count):
        columns = slice(head_index * HEAD_DIM, (head_index + 1) * HEAD_DIM)
        grad_head = attended_grad[:, columns]
        dprobs = contract_last(grad_head, value_flat[:, columns])
        dscores = (
            weights_list[head_index].astype(jnp.float32)
            * (dprobs - delta_list[head_index][:, None])
            * score_scale
        ).astype(jnp.bfloat16)
        query_grads.append(
            jnp.dot(dscores, key_flat[:, columns], preferred_element_type=jnp.float32).astype(
                jnp.bfloat16
            )
        )
        key_parts.append(contract_first(dscores, query_rows[:, columns]))
        value_parts.append(contract_first(weights_list[head_index], grad_head))
    grad_queries = jnp.concatenate(query_grads, 1)
    key_partial = lax.optimization_barrier(
        jnp.concatenate(key_parts, 1).reshape(9, row_count, column_count).astype(jnp.bfloat16)
    )
    value_partial = lax.optimization_barrier(
        jnp.concatenate(value_parts, 1).reshape(9, row_count, column_count).astype(jnp.bfloat16)
    )

    def shift_back(pieces, distance):
        return jax.tree.map(
            lambda part, own: part.astype(own.dtype),
            shifted(as_sent(pieces), "tok", distance),
            pieces,
        )

    grad_keys, grad_values = return_each((key_partial, value_partial), shift_back, GRID_W)
    return (
        attended,
        grad_queries,
        grad_keys.astype(jnp.bfloat16),
        grad_values.astype(jnp.bfloat16),
    )


def solution(mesh):
    in_specs = (
        P("tok", "head"),
        P("tok", "head"),
        P("tok", "head"),
        P(),
        P("head", None),
        P(("tok", "head"), None),
    )
    out_specs = (P("tok", "head"), P("tok", "head"), P("tok", "head"), P("tok", "head"))
    return jax.shard_map(local, mesh=mesh, in_specs=in_specs, out_specs=out_specs, check_vma=False)
```

profile of v0, /device:TPU:458, one launch (start us, length us, event | category | flops | bytes accessed | tf_op | source)
XLA Modules:
  0.0 213.7 jit_solution(13035924788157134013)
XLA Ops:
  7.2 6.4 %collective-permute-start = (bf16[192,384]{1,0:T(8,128)(2,1)}, bf16[192,384]{1,0:T(8,128)(2,1)}, u32[]{:S(2)}, u32[]{:S(2)}) collective-permute-start(bf16[192,384]{1,0:T(8,128)(2,1)} %param.7), channel_id=1, source_target_pairs={{0,36},{4,40},{8,44},{12,48},{16,52},{20,56},{24,60},{28,64},{32,6... | collective-permute-start | bytes 442376 | tf_op jit(solution)/shard_map/ppermute | solution.py:20
  13.7 1.9 collective-permute-start.1
  15.6 1.9 collective-permute-start.2
  17.5 1.9 collective-permute-start.3
  19.5 3.6 %collective-permute-start.4 = (bf16[192,384]{1,0:T(8,128)(2,1)}, bf16[192,384]{1,0:T(8,128)(2,1)S(1)}, u32[]{:S(2)}, u32[]{:S(2)}) collective-permute-start(bf16[192,384]{1,0:T(8,128)(2,1)} %param.7), channel_id=1, source_target_pairs={{4,0},{8,4},{12,8},{16,12},{20,16},{24,20},{28,24},{32,28},{36,32}... | collective-permute-start | bytes 442376 | tf_op jit(solution)/shard_map/ppermute | solution.py:20
  23.2 0.8 constant_dynamic-slice_fusion
  24.0 0.7 gather_fusion
  24.8 0.7 collective-permute-done
  25.6 6.8 %collective-permute-start.5 = (bf16[192,384]{1,0:T(8,128)(2,1)}, bf16[192,384]{1,0:T(8,128)(2,1)S(1)}, u32[]{:S(2)}, u32[]{:S(2)}) collective-permute-start(bf16[192,384]{1,0:T(8,128)(2,1)} %param.7), channel_id=1, source_target_pairs={{28,0},{32,4},{36,8},{40,12},{44,16},{48,20},{52,24},{56,28},{60,3... | collective-permute-start | bytes 442376 | tf_op jit(solution)/shard_map/ppermute | solution.py:20
  32.4 0.9 bitcast_dynamic-update-slice_fusion.17
  33.3 9.7 %collective-permute-start.6 = (bf16[192,384]{1,0:T(8,128)(2,1)}, bf16[192,384]{1,0:T(8,128)(2,1)S(1)}, u32[]{:S(2)}, u32[]{:S(2)}) collective-permute-start(bf16[192,384]{1,0:T(8,128)(2,1)} %param.7), channel_id=1, source_target_pairs={{32,0},{36,4},{40,8},{44,12},{48,16},{52,20},{56,24},{60,28},{64,3... | collective-permute-start | bytes 442376 | tf_op jit(solution)/shard_map/ppermute | solution.py:20
  43.1 6.3 %collective-permute-start.7 = (bf16[192,384]{1,0:T(8,128)(2,1)S(1)}, bf16[192,384]{1,0:T(8,128)(2,1)S(1)}, u32[]{:S(2)}, u32[]{:S(2)}) collective-permute-start(bf16[192,384]{1,0:T(8,128)(2,1)S(1)} %copy-done.5), channel_id=1, source_target_pairs={{36,0},{40,4},{44,8},{48,12},{52,16},{56,20},{60,24},{64,28},{68,3... | collective-permute-start | bytes 442376 | tf_op jit(solution)/shard_map/ppermute | solution.py:20
  49.4 3.2 %collective-permute-start.8 = (bf16[192,384]{1,0:T(8,128)(2,1)S(1)}, bf16[192,384]{1,0:T(8,128)(2,1)S(1)}, u32[]{:S(2)}, u32[]{:S(2)}) collective-permute-start(bf16[192,384]{1,0:T(8,128)(2,1)S(1)} %copy-done.6), channel_id=1, source_target_pairs={{0,36},{4,40},{8,44},{12,48},{16,52},{20,56},{24,60},{28,64},{32,6... | collective-permute-start | bytes 442376 | tf_op jit(solution)/shard_map/ppermute | solution.py:20
  52.7 1.9 collective-permute-start.9
  54.6 1.9 collective-permute-start.10
  56.6 1.9 collective-permute-start.11
  58.6 5.2 %collective-permute-done.7 = bf16[192,384]{1,0:T(8,128)(2,1)S(1)} collective-permute-done((bf16[192,384]{1,0:T(8,128)(2,1)S(1)}, bf16[192,384]{1,0:T(8,128)(2,1)S(1)}, u32[]{:S(2)}, u32[]{:S(2)}) %collective-permute-start.7) | collective-permute-done | bytes 147488 | tf_op jit(solution)/shard_map/ppermute | solution.py:20
  63.7 11.7 %collective-permute-start.12 = (bf16[192,384]{1,0:T(8,128)(2,1)S(1)}, bf16[192,384]{1,0:T(8,128)(2,1)S(1)}, u32[]{:S(2)}, u32[]{:S(2)}) collective-permute-start(bf16[192,384]{1,0:T(8,128)(2,1)S(1)} %copy-done.6), channel_id=1, source_target_pairs={{4,0},{8,4},{12,8},{16,12},{20,16},{24,20},{28,24},{32,28},{36,32}... | collective-permute-start | bytes 442376 | tf_op jit(solution)/shard_map/ppermute | solution.py:20
  75.5 0.4 fusion.54
  76.0 0.4 fusion.53
  76.4 0.3 exponential_reduce_fusion.1
  77.0 0.4 fusion.52
  77.5 8.1 %collective-permute-start.13 = (bf16[192,384]{1,0:T(8,128)(2,1)S(1)}, bf16[192,384]{1,0:T(8,128)(2,1)S(1)}, u32[]{:S(2)}, u32[]{:S(2)}) collective-permute-start(bf16[192,384]{1,0:T(8,128)(2,1)S(1)} %copy-done.6), channel_id=1, source_target_pairs={{28,0},{32,4},{36,8},{40,12},{44,16},{48,20},{52,24},{56,28},{60,3... | collective-permute-start | bytes 442376 | tf_op jit(solution)/shard_map/ppermute | solution.py:20
  85.7 7.9 %collective-permute-start.14 = (bf16[192,384]{1,0:T(8,128)(2,1)S(1)}, bf16[192,384]{1,0:T(8,128)(2,1)S(1)}, u32[]{:S(2)}, u32[]{:S(2)}) collective-permute-start(bf16[192,384]{1,0:T(8,128)(2,1)S(1)} %copy-done.6), channel_id=1, source_target_pairs={{32,0},{36,4},{40,8},{44,12},{48,16},{52,20},{56,24},{60,28},{64,3... | collective-permute-start | bytes 442376 | tf_op jit(solution)/shard_map/ppermute | solution.py:20
  93.7 1.9 collective-permute-start.15
  96.5 1.3 collective-permute-done.14
  97.8 6.2 %collective-permute-done.15 = bf16[192,384]{1,0:T(8,128)(2,1)S(1)} collective-permute-done((bf16[192,384]{1,0:T(8,128)(2,1)S(1)}, bf16[192,384]{1,0:T(8,128)(2,1)S(1)}, u32[]{:S(2)}, u32[]{:S(2)}) %collective-permute-start.15) | collective-permute-done | bytes 147488 | tf_op jit(solution)/shard_map/ppermute | solution.py:20
  104.7 0.5 copy-done.9
  105.1 0.9 copy-done.1
  106.3 1.1 exponential_convert_fusion.2
  107.5 2.2 %convolution_convert_fusion.6 = bf16[192,384]{1,0:T(8,128)(2,1)S(1)} fusion(bf16[192,3072]{1,0:T(8,128)(2,1)} %all-gather.2.cloned.1.call-done, bf16[384,3072]{1,0:T(8,128)(2,1)S(1)} %copy-done), kind=kOutput, calls=%fused_computation.33 | convolution fusion | flops 453058560 | bytes 3686400 | tf_op jit(solution)/shard_map/dot_general | solution.py:68
  109.7 0.5 convolution_convert_fusion.1
  110.2 0.6 copy-done.2
  110.8 0.5 convolution_convert_fusion
  111.3 0.5 convolution_convert_fusion.2
  112.1 2.8 %collective-permute-start.24 = (bf16[192,384]{1,0:T(8,128)(2,1)S(1)}, bf16[192,384]{1,0:T(8,128)(2,1)S(1)}, u32[]{:S(2)}, u32[]{:S(2)}) collective-permute-start(bf16[192,384]{1,0:T(8,128)(2,1)S(1)} %get-tuple-element.7), channel_id=1, source_target_pairs={{36,0},{40,4},{44,8},{48,12},{52,16},{56,20},{60,24},{64,28},{68,3... | collective-permute-start | bytes 442376 | tf_op jit(solution)/shard_map/ppermute | solution.py:20
  114.8 5.8 %collective-permute-start.25 = (bf16[192,384]{1,0:T(8,128)(2,1)S(1)}, bf16[192,384]{1,0:T(8,128)(2,1)S(1)}, u32[]{:S(2)}, u32[]{:S(2)}) collective-permute-start(bf16[192,384]{1,0:T(8,128)(2,1)S(1)} %get-tuple-element.14), channel_id=1, source_target_pairs={{32,0},{36,4},{40,8},{44,12},{48,16},{52,20},{56,24},{60,28},{64,3... | collective-permute-start | bytes 442376 | tf_op jit(solution)/shard_map/ppermute | solution.py:20
  120.7 3.5 %collective-permute-start.26 = (bf16[192,384]{1,0:T(8,128)(2,1)S(1)}, bf16[192,384]{1,0:T(8,128)(2,1)S(1)}, u32[]{:S(2)}, u32[]{:S(2)}) collective-permute-start(bf16[192,384]{1,0:T(8,128)(2,1)S(1)} %get-tuple-element.13), channel_id=1, source_target_pairs={{28,0},{32,4},{36,8},{40,12},{44,16},{48,20},{52,24},{56,28},{60,3... | collective-permute-start | bytes 442376 | tf_op jit(solution)/shard_map/ppermute | solution.py:20
  124.2 1.9 collective-permute-start.27
  126.1 3.0 %collective-permute-start.28 = (bf16[192,384]{1,0:T(8,128)(2,1)S(1)}, bf16[192,384]{1,0:T(8,128)(2,1)S(1)}, u32[]{:S(2)}, u32[]{:S(2)}) collective-permute-start(bf16[192,384]{1,0:T(8,128)(2,1)S(1)} %get-tuple-element.11), channel_id=1, source_target_pairs={{0,4},{4,8},{8,12},{12,16},{16,20},{20,24},{24,28},{28,32},{32,36}... | collective-permute-start | bytes 442376 | tf_op jit(solution)/shard_map/ppermute | solution.py:20
  129.2 0.5 multiply_reduce_fusion.2
  129.6 0.4 fusion.11
  130.0 0.5 convolution_convert_fusion.5
  130.5 0.4 fusion.10
  130.9 0.5 convolution_convert_fusion.4
  131.4 0.4 fusion.9
  131.7 0.5 convolution_convert_fusion.3
  132.6 1.2 copy-done.8
  134.1 5.7 %collective-permute-start.29 = (bf16[192,384]{1,0:T(8,128)(2,1)S(1)}, bf16[192,384]{1,0:T(8,128)(2,1)S(1)}, u32[]{:S(2)}, u32[]{:S(2)}) collective-permute-start(bf16[192,384]{1,0:T(8,128)(2,1)S(1)} %get-tuple-element.10), channel_id=1, source_target_pairs={{0,28},{4,32},{8,36},{12,40},{16,44},{20,48},{24,52},{28,56},{32,6... | collective-permute-start | bytes 442376 | tf_op jit(solution)/shard_map/ppermute | solution.py:20
  140.1 1.9 collective-permute-start.30
  142.1 2.5 %collective-permute-start.31 = (bf16[192,384]{1,0:T(8,128)(2,1)S(1)}, bf16[192,384]{1,0:T(8,128)(2,1)S(1)}, u32[]{:S(2)}, u32[]{:S(2)}) collective-permute-start(bf16[192,384]{1,0:T(8,128)(2,1)S(1)} %get-tuple-element.8), channel_id=1, source_target_pairs={{0,36},{4,40},{8,44},{12,48},{16,52},{20,56},{24,60},{28,64},{32,6... | collective-permute-start | bytes 442376 | tf_op jit(solution)/shard_map/ppermute | solution.py:20
  144.6 6.9 %collective-permute-start.16 = (bf16[192,384]{1,0:T(8,128)(2,1)S(1)}, bf16[192,384]{1,0:T(8,128)(2,1)S(1)}, u32[]{:S(2)}, u32[]{:S(2)}) collective-permute-start(bf16[192,384]{1,0:T(8,128)(2,1)S(1)} %get-tuple-element.15), channel_id=1, source_target_pairs={{36,0},{40,4},{44,8},{48,12},{52,16},{56,20},{60,24},{64,28},{68,3... | collective-permute-start | bytes 442376 | tf_op jit(solution)/shard_map/ppermute | solution.py:20
  151.6 7.8 %collective-permute-start.17 = (bf16[192,384]{1,0:T(8,128)(2,1)S(1)}, bf16[192,384]{1,0:T(8,128)(2,1)S(1)}, u32[]{:S(2)}, u32[]{:S(2)}) collective-permute-start(bf16[192,384]{1,0:T(8,128)(2,1)S(1)} %get-tuple-element.22), channel_id=1, source_target_pairs={{32,0},{36,4},{40,8},{44,12},{48,16},{52,20},{56,24},{60,28},{64,3... | collective-permute-start | bytes 442376 | tf_op jit(solution)/shard_map/ppermute | solution.py:20
  159.4 5.0 %collective-permute-start.18 = (bf16[192,384]{1,0:T(8,128)(2,1)S(1)}, bf16[192,384]{1,0:T(8,128)(2,1)S(1)}, u32[]{:S(2)}, u32[]{:S(2)}) collective-permute-start(bf16[192,384]{1,0:T(8,128)(2,1)S(1)} %get-tuple-element.21), channel_id=1, source_target_pairs={{28,0},{32,4},{36,8},{40,12},{44,16},{48,20},{52,24},{56,28},{60,3... | collective-permute-start | bytes 442376 | tf_op jit(solution)/shard_map/ppermute | solution.py:20
  164.8 0.8 pad_maximum_fusion.2
  165.6 2.8 %collective-permute-start.19 = (bf16[192,384]{1,0:T(8,128)(2,1)S(1)}, bf16[192,384]{1,0:T(8,128)(2,1)S(1)}, u32[]{:S(2)}, u32[]{:S(2)}) collective-permute-start(bf16[192,384]{1,0:T(8,128)(2,1)S(1)} %get-tuple-element.20), channel_id=1, source_target_pairs={{4,0},{8,4},{12,8},{16,12},{20,16},{24,20},{28,24},{32,28},{36,32}... | collective-permute-start | bytes 442376 | tf_op jit(solution)/shard_map/ppermute | solution.py:20
  168.3 1.9 collective-permute-start.20
  170.3 14.9 %collective-permute-start.21 = (bf16[192,384]{1,0:T(8,128)(2,1)S(1)}, bf16[192,384]{1,0:T(8,128)(2,1)S(1)}, u32[]{:S(2)}, u32[]{:S(2)}) collective-permute-start(bf16[192,384]{1,0:T(8,128)(2,1)S(1)} %get-tuple-element.18), channel_id=1, source_target_pairs={{0,28},{4,32},{8,36},{12,40},{16,44},{20,48},{24,52},{28,56},{32,6... | collective-permute-start | bytes 442376 | tf_op jit(solution)/shard_map/ppermute | solution.py:20
  185.1 1.9 collective-permute-start.22
  187.1 1.9 collective-permute-start.23
  189.0 0.8 fusion.31
  189.9 13.1 %collective-permute-done.22 = bf16[192,384]{1,0:T(8,128)(2,1)S(1)} collective-permute-done((bf16[192,384]{1,0:T(8,128)(2,1)S(1)}, bf16[192,384]{1,0:T(8,128)(2,1)S(1)}, u32[]{:S(2)}, u32[]{:S(2)}) %collective-permute-start.22) | collective-permute-done | bytes 147488 | tf_op jit(solution)/shard_map/ppermute | solution.py:20
  202.9 3.1 %collective-permute-done.23 = bf16[192,384]{1,0:T(8,128)(2,1)S(1)} collective-permute-done((bf16[192,384]{1,0:T(8,128)(2,1)S(1)}, bf16[192,384]{1,0:T(8,128)(2,1)S(1)}, u32[]{:S(2)}, u32[]{:S(2)}) %collective-permute-start.23) | collective-permute-done | bytes 147488 | tf_op jit(solution)/shard_map/ppermute | solution.py:20
  206.0 0.8 fusion.39
  (86 shorter events, 4.3 us)
Async XLA Ops:
  7.2 100.3 %copy-start = (bf16[384,3072]{1,0:T(8,128)(2,1)S(1)}, bf16[384,3072]{1,0:T(8,128)(2,1)}, u32[]{:S(2)}) copy-start(bf16[384,3072]{1,0:T(8,128)(2,1)} %param.10) | copy-start | bytes 7077892
  7.2 35.9 %copy-start.5 = (bf16[192,384]{1,0:T(8,128)(2,1)S(1)}, bf16[192,384]{1,0:T(8,128)(2,1)}, u32[]{:S(2)}) copy-start(bf16[192,384]{1,0:T(8,128)(2,1)} %param.7) | copy-start | bytes 442372
  7.2 42.2 %copy-start.6 = (bf16[192,384]{1,0:T(8,128)(2,1)S(1)}, bf16[192,384]{1,0:T(8,128)(2,1)}, u32[]{:S(2)}) copy-start(bf16[192,384]{1,0:T(8,128)(2,1)} %param.8) | copy-start | bytes 442372
  7.2 100.2 %all-gather.2.cloned.1.call-start = ((), (), s32[]{:S(2)}) async-start(), calls=%async_computation | async-start | bytes 1474560 | tf_op jit(solution)/shard_map/all_gather | solution.py:119
  7.2 18.3 %collective-permute-start = (bf16[192,384]{1,0:T(8,128)(2,1)}, bf16[192,384]{1,0:T(8,128)(2,1)}, u32[]{:S(2)}, u32[]{:S(2)}) collective-permute-start(bf16[192,384]{1,0:T(8,128)(2,1)} %param.7), channel_id=1, source_target_pairs={{0,36},{4,40},{8,44},{12,48},{16,52},{20,56},{24,60},{28,64},{32,6... | collective-permute-start | bytes 442376 | tf_op jit(solution)/shard_map/ppermute | solution.py:20
  13.7 19.6 %collective-permute-start.1 = (bf16[192,384]{1,0:T(8,128)(2,1)}, bf16[192,384]{1,0:T(8,128)(2,1)S(1)}, u32[]{:S(2)}, u32[]{:S(2)}) collective-permute-start(bf16[192,384]{1,0:T(8,128)(2,1)} %param.7), channel_id=1, source_target_pairs={{0,32},{4,36},{8,40},{12,44},{16,48},{20,52},{24,56},{28,60},{32,6... | collective-permute-start | bytes 442376 | tf_op jit(solution)/shard_map/ppermute | solution.py:20
  15.6 27.4 %collective-permute-start.2 = (bf16[192,384]{1,0:T(8,128)(2,1)}, bf16[192,384]{1,0:T(8,128)(2,1)S(1)}, u32[]{:S(2)}, u32[]{:S(2)}) collective-permute-start(bf16[192,384]{1,0:T(8,128)(2,1)} %param.7), channel_id=1, source_target_pairs={{0,28},{4,32},{8,36},{12,40},{16,44},{20,48},{24,52},{28,56},{32,6... | collective-permute-start | bytes 442376 | tf_op jit(solution)/shard_map/ppermute | solution.py:20
  17.5 31.8 %collective-permute-start.3 = (bf16[192,384]{1,0:T(8,128)(2,1)}, bf16[192,384]{1,0:T(8,128)(2,1)S(1)}, u32[]{:S(2)}, u32[]{:S(2)}) collective-permute-start(bf16[192,384]{1,0:T(8,128)(2,1)} %param.7), channel_id=1, source_target_pairs={{0,4},{4,8},{8,12},{12,16},{16,20},{20,24},{24,28},{28,32},{32,36}... | collective-permute-start | bytes 442376 | tf_op jit(solution)/shard_map/ppermute | solution.py:20
  19.5 33.2 %collective-permute-start.4 = (bf16[192,384]{1,0:T(8,128)(2,1)}, bf16[192,384]{1,0:T(8,128)(2,1)S(1)}, u32[]{:S(2)}, u32[]{:S(2)}) collective-permute-start(bf16[192,384]{1,0:T(8,128)(2,1)} %param.7), channel_id=1, source_target_pairs={{4,0},{8,4},{12,8},{16,12},{20,16},{24,20},{28,24},{32,28},{36,32}... | collective-permute-start | bytes 442376 | tf_op jit(solution)/shard_map/ppermute | solution.py:20
  24.8 50.7 %copy-start.4 = (bf16[192,384]{1,0:T(8,128)(2,1)S(1)}, bf16[192,384]{1,0:T(8,128)(2,1)}, u32[]{:S(2)}) copy-start(bf16[192,384]{1,0:T(8,128)(2,1)} %param.6) | copy-start | bytes 442372
  25.6 29.1 %collective-permute-start.5 = (bf16[192,384]{1,0:T(8,128)(2,1)}, bf16[192,384]{1,0:T(8,128)(2,1)S(1)}, u32[]{:S(2)}, u32[]{:S(2)}) collective-permute-start(bf16[192,384]{1,0:T(8,128)(2,1)} %param.7), channel_id=1, source_target_pairs={{28,0},{32,4},{36,8},{40,12},{44,16},{48,20},{52,24},{56,28},{60,3... | collective-permute-start | bytes 442376 | tf_op jit(solution)/shard_map/ppermute | solution.py:20
  33.3 23.3 %collective-permute-start.6 = (bf16[192,384]{1,0:T(8,128)(2,1)}, bf16[192,384]{1,0:T(8,128)(2,1)S(1)}, u32[]{:S(2)}, u32[]{:S(2)}) collective-permute-start(bf16[192,384]{1,0:T(8,128)(2,1)} %param.7), channel_id=1, source_target_pairs={{32,0},{36,4},{40,8},{44,12},{48,16},{52,20},{56,24},{60,28},{64,3... | collective-permute-start | bytes 442376 | tf_op jit(solution)/shard_map/ppermute | solution.py:20
  43.1 20.7 %collective-permute-start.7 = (bf16[192,384]{1,0:T(8,128)(2,1)S(1)}, bf16[192,384]{1,0:T(8,128)(2,1)S(1)}, u32[]{:S(2)}, u32[]{:S(2)}) collective-permute-start(bf16[192,384]{1,0:T(8,128)(2,1)S(1)} %copy-done.5), channel_id=1, source_target_pairs={{36,0},{40,4},{44,8},{48,12},{52,16},{56,20},{60,24},{64,28},{68,3... | collective-permute-start | bytes 442376 | tf_op jit(solution)/shard_map/ppermute | solution.py:20
  49.4 28.1 %collective-permute-start.8 = (bf16[192,384]{1,0:T(8,128)(2,1)S(1)}, bf16[192,384]{1,0:T(8,128)(2,1)S(1)}, u32[]{:S(2)}, u32[]{:S(2)}) collective-permute-start(bf16[192,384]{1,0:T(8,128)(2,1)S(1)} %copy-done.6), channel_id=1, source_target_pairs={{0,36},{4,40},{8,44},{12,48},{16,52},{20,56},{24,60},{28,64},{32,6... | collective-permute-start | bytes 442376 | tf_op jit(solution)/shard_map/ppermute | solution.py:20
  52.7 33.0 %collective-permute-start.9 = (bf16[192,384]{1,0:T(8,128)(2,1)S(1)}, bf16[192,384]{1,0:T(8,128)(2,1)S(1)}, u32[]{:S(2)}, u32[]{:S(2)}) collective-permute-start(bf16[192,384]{1,0:T(8,128)(2,1)S(1)} %copy-done.6), channel_id=1, source_target_pairs={{0,32},{4,36},{8,40},{12,44},{16,48},{20,52},{24,56},{28,60},{32,6... | collective-permute-start | bytes 442376 | tf_op jit(solution)/shard_map/ppermute | solution.py:20
  54.6 39.0 %collective-permute-start.10 = (bf16[192,384]{1,0:T(8,128)(2,1)S(1)}, bf16[192,384]{1,0:T(8,128)(2,1)S(1)}, u32[]{:S(2)}, u32[]{:S(2)}) collective-permute-start(bf16[192,384]{1,0:T(8,128)(2,1)S(1)} %copy-done.6), channel_id=1, source_target_pairs={{0,28},{4,32},{8,36},{12,40},{16,44},{20,48},{24,52},{28,56},{32,6... | collective-permute-start | bytes 442376 | tf_op jit(solution)/shard_map/ppermute | solution.py:20
  56.6 39.0 %collective-permute-start.11 = (bf16[192,384]{1,0:T(8,128)(2,1)S(1)}, bf16[192,384]{1,0:T(8,128)(2,1)S(1)}, u32[]{:S(2)}, u32[]{:S(2)}) collective-permute-start(bf16[192,384]{1,0:T(8,128)(2,1)S(1)} %copy-done.6), channel_id=1, source_target_pairs={{0,4},{4,8},{8,12},{12,16},{16,20},{20,24},{24,28},{28,32},{32,36}... | collective-permute-start | bytes 442376 | tf_op jit(solution)/shard_map/ppermute | solution.py:20
  63.7 32.3 %collective-permute-start.12 = (bf16[192,384]{1,0:T(8,128)(2,1)S(1)}, bf16[192,384]{1,0:T(8,128)(2,1)S(1)}, u32[]{:S(2)}, u32[]{:S(2)}) collective-permute-start(bf16[192,384]{1,0:T(8,128)(2,1)S(1)} %copy-done.6), channel_id=1, source_target_pairs={{4,0},{8,4},{12,8},{16,12},{20,16},{24,20},{28,24},{32,28},{36,32}... | collective-permute-start | bytes 442376 | tf_op jit(solution)/shard_map/ppermute | solution.py:20
  75.5 1.5 copy-start.7
  77.5 18.6 %collective-permute-start.13 = (bf16[192,384]{1,0:T(8,128)(2,1)S(1)}, bf16[192,384]{1,0:T(8,128)(2,1)S(1)}, u32[]{:S(2)}, u32[]{:S(2)}) collective-permute-start(bf16[192,384]{1,0:T(8,128)(2,1)S(1)} %copy-done.6), channel_id=1, source_target_pairs={{28,0},{32,4},{36,8},{40,12},{44,16},{48,20},{52,24},{56,28},{60,3... | collective-permute-start | bytes 442376 | tf_op jit(solution)/shard_map/ppermute | solution.py:20
  85.7 12.1 %collective-permute-start.14 = (bf16[192,384]{1,0:T(8,128)(2,1)S(1)}, bf16[192,384]{1,0:T(8,128)(2,1)S(1)}, u32[]{:S(2)}, u32[]{:S(2)}) collective-permute-start(bf16[192,384]{1,0:T(8,128)(2,1)S(1)} %copy-done.6), channel_id=1, source_target_pairs={{32,0},{36,4},{40,8},{44,12},{48,16},{52,20},{56,24},{60,28},{64,3... | collective-permute-start | bytes 442376 | tf_op jit(solution)/shard_map/ppermute | solution.py:20
  93.7 10.4 %collective-permute-start.15 = (bf16[192,384]{1,0:T(8,128)(2,1)S(1)}, bf16[192,384]{1,0:T(8,128)(2,1)S(1)}, u32[]{:S(2)}, u32[]{:S(2)}) collective-permute-start(bf16[192,384]{1,0:T(8,128)(2,1)S(1)} %copy-done.6), channel_id=1, source_target_pairs={{36,0},{40,4},{44,8},{48,12},{52,16},{56,20},{60,24},{64,28},{68,3... | collective-permute-start | bytes 442376 | tf_op jit(solution)/shard_map/ppermute | solution.py:20
  104.1 1.1 copy-start.9
  105.1 0.9 copy-start.1
  109.7 1.1 copy-start.2
  109.7 1.6 copy-start.3
  111.9 17.3 %copy-start.10 = (bf16[9,192,384]{2,1,0:T(8,128)(2,1)S(1)}, bf16[9,192,384]{2,1,0:T(8,128)(2,1)}, u32[]{:S(2)}) copy-start(bf16[9,192,384]{2,1,0:T(8,128)(2,1)} %copy-done.9) | copy-start | bytes 3981316
  112.1 22.0 %collective-permute-start.24 = (bf16[192,384]{1,0:T(8,128)(2,1)S(1)}, bf16[192,384]{1,0:T(8,128)(2,1)S(1)}, u32[]{:S(2)}, u32[]{:S(2)}) collective-permute-start(bf16[192,384]{1,0:T(8,128)(2,1)S(1)} %get-tuple-element.7), channel_id=1, source_target_pairs={{36,0},{40,4},{44,8},{48,12},{52,16},{56,20},{60,24},{64,28},{68,3... | collective-permute-start | bytes 442376 | tf_op jit(solution)/shard_map/ppermute | solution.py:20
  114.8 25.3 %collective-permute-start.25 = (bf16[192,384]{1,0:T(8,128)(2,1)S(1)}, bf16[192,384]{1,0:T(8,128)(2,1)S(1)}, u32[]{:S(2)}, u32[]{:S(2)}) collective-permute-start(bf16[192,384]{1,0:T(8,128)(2,1)S(1)} %get-tuple-element.14), channel_id=1, source_target_pairs={{32,0},{36,4},{40,8},{44,12},{48,16},{52,20},{56,24},{60,28},{64,3... | collective-permute-start | bytes 442376 | tf_op jit(solution)/shard_map/ppermute | solution.py:20
  120.7 21.4 %collective-permute-start.26 = (bf16[192,384]{1,0:T(8,128)(2,1)S(1)}, bf16[192,384]{1,0:T(8,128)(2,1)S(1)}, u32[]{:S(2)}, u32[]{:S(2)}) collective-permute-start(bf16[192,384]{1,0:T(8,128)(2,1)S(1)} %get-tuple-element.13), channel_id=1, source_target_pairs={{28,0},{32,4},{36,8},{40,12},{44,16},{48,20},{52,24},{56,28},{60,3... | collective-permute-start | bytes 442376 | tf_op jit(solution)/shard_map/ppermute | solution.py:20
  124.2 20.4 %collective-permute-start.27 = (bf16[192,384]{1,0:T(8,128)(2,1)S(1)}, bf16[192,384]{1,0:T(8,128)(2,1)S(1)}, u32[]{:S(2)}, u32[]{:S(2)}) collective-permute-start(bf16[192,384]{1,0:T(8,128)(2,1)S(1)} %get-tuple-element.12), channel_id=1, source_target_pairs={{4,0},{8,4},{12,8},{16,12},{20,16},{24,20},{28,24},{32,28},{36,32}... | collective-permute-start | bytes 442376 | tf_op jit(solution)/shard_map/ppermute | solution.py:20
  126.1 25.4 %collective-permute-start.28 = (bf16[192,384]{1,0:T(8,128)(2,1)S(1)}, bf16[192,384]{1,0:T(8,128)(2,1)S(1)}, u32[]{:S(2)}, u32[]{:S(2)}) collective-permute-start(bf16[192,384]{1,0:T(8,128)(2,1)S(1)} %get-tuple-element.11), channel_id=1, source_target_pairs={{0,4},{4,8},{8,12},{12,16},{16,20},{20,24},{24,28},{28,32},{32,36}... | collective-permute-start | bytes 442376 | tf_op jit(solution)/shard_map/ppermute | solution.py:20
  132.4 1.3 copy-start.8
  134.1 25.3 %collective-permute-start.29 = (bf16[192,384]{1,0:T(8,128)(2,1)S(1)}, bf16[192,384]{1,0:T(8,128)(2,1)S(1)}, u32[]{:S(2)}, u32[]{:S(2)}) collective-permute-start(bf16[192,384]{1,0:T(8,128)(2,1)S(1)} %get-tuple-element.10), channel_id=1, source_target_pairs={{0,28},{4,32},{8,36},{12,40},{16,44},{20,48},{24,52},{28,56},{32,6... | collective-permute-start | bytes 442376 | tf_op jit(solution)/shard_map/ppermute | solution.py:20
  140.1 25.4 %collective-permute-start.30 = (bf16[192,384]{1,0:T(8,128)(2,1)S(1)}, bf16[192,384]{1,0:T(8,128)(2,1)S(1)}, u32[]{:S(2)}, u32[]{:S(2)}) collective-permute-start(bf16[192,384]{1,0:T(8,128)(2,1)S(1)} %get-tuple-element.9), channel_id=1, source_target_pairs={{0,32},{4,36},{8,40},{12,44},{16,48},{20,52},{24,56},{28,60},{32,6... | collective-permute-start | bytes 442376 | tf_op jit(solution)/shard_map/ppermute | solution.py:20
  142.1 26.3 %collective-permute-start.31 = (bf16[192,384]{1,0:T(8,128)(2,1)S(1)}, bf16[192,384]{1,0:T(8,128)(2,1)S(1)}, u32[]{:S(2)}, u32[]{:S(2)}) collective-permute-start(bf16[192,384]{1,0:T(8,128)(2,1)S(1)} %get-tuple-element.8), channel_id=1, source_target_pairs={{0,36},{4,40},{8,44},{12,48},{16,52},{20,56},{24,60},{28,64},{32,6... | collective-permute-start | bytes 442376 | tf_op jit(solution)/shard_map/ppermute | solution.py:20
  144.6 25.6 %collective-permute-start.16 = (bf16[192,384]{1,0:T(8,128)(2,1)S(1)}, bf16[192,384]{1,0:T(8,128)(2,1)S(1)}, u32[]{:S(2)}, u32[]{:S(2)}) collective-permute-start(bf16[192,384]{1,0:T(8,128)(2,1)S(1)} %get-tuple-element.15), channel_id=1, source_target_pairs={{36,0},{40,4},{44,8},{48,12},{52,16},{56,20},{60,24},{64,28},{68,3... | collective-permute-start | bytes 442376 | tf_op jit(solution)/shard_map/ppermute | solution.py:20
  151.6 33.6 %collective-permute-start.17 = (bf16[192,384]{1,0:T(8,128)(2,1)S(1)}, bf16[192,384]{1,0:T(8,128)(2,1)S(1)}, u32[]{:S(2)}, u32[]{:S(2)}) collective-permute-start(bf16[192,384]{1,0:T(8,128)(2,1)S(1)} %get-tuple-element.22), channel_id=1, source_target_pairs={{32,0},{36,4},{40,8},{44,12},{48,16},{52,20},{56,24},{60,28},{64,3... | collective-permute-start | bytes 442376 | tf_op jit(solution)/shard_map/ppermute | solution.py:20
  159.4 27.7 %collective-permute-start.18 = (bf16[192,384]{1,0:T(8,128)(2,1)S(1)}, bf16[192,384]{1,0:T(8,128)(2,1)S(1)}, u32[]{:S(2)}, u32[]{:S(2)}) collective-permute-start(bf16[192,384]{1,0:T(8,128)(2,1)S(1)} %get-tuple-element.21), channel_id=1, source_target_pairs={{28,0},{32,4},{36,8},{40,12},{44,16},{48,20},{52,24},{56,28},{60,3... | collective-permute-start | bytes 442376 | tf_op jit(solution)/shard_map/ppermute | solution.py:20
  165.6 24.3 %collective-permute-start.19 = (bf16[192,384]{1,0:T(8,128)(2,1)S(1)}, bf16[192,384]{1,0:T(8,128)(2,1)S(1)}, u32[]{:S(2)}, u32[]{:S(2)}) collective-permute-start(bf16[192,384]{1,0:T(8,128)(2,1)S(1)} %get-tuple-element.20), channel_id=1, source_target_pairs={{4,0},{8,4},{12,8},{16,12},{20,16},{24,20},{28,24},{32,28},{36,32}... | collective-permute-start | bytes 442376 | tf_op jit(solution)/shard_map/ppermute | solution.py:20
  168.3 21.5 %collective-permute-start.20 = (bf16[192,384]{1,0:T(8,128)(2,1)S(1)}, bf16[192,384]{1,0:T(8,128)(2,1)S(1)}, u32[]{:S(2)}, u32[]{:S(2)}) collective-permute-start(bf16[192,384]{1,0:T(8,128)(2,1)S(1)} %get-tuple-element.19), channel_id=1, source_target_pairs={{0,4},{4,8},{8,12},{12,16},{16,20},{20,24},{24,28},{28,32},{32,36}... | collective-permute-start | bytes 442376 | tf_op jit(solution)/shard_map/ppermute | solution.py:20
  170.3 19.6 %collective-permute-start.21 = (bf16[192,384]{1,0:T(8,128)(2,1)S(1)}, bf16[192,384]{1,0:T(8,128)(2,1)S(1)}, u32[]{:S(2)}, u32[]{:S(2)}) collective-permute-start(bf16[192,384]{1,0:T(8,128)(2,1)S(1)} %get-tuple-element.18), channel_id=1, source_target_pairs={{0,28},{4,32},{8,36},{12,40},{16,44},{20,48},{24,52},{28,56},{32,6... | collective-permute-start | bytes 442376 | tf_op jit(solution)/shard_map/ppermute | solution.py:20
  185.1 17.8 %collective-permute-start.22 = (bf16[192,384]{1,0:T(8,128)(2,1)S(1)}, bf16[192,384]{1,0:T(8,128)(2,1)S(1)}, u32[]{:S(2)}, u32[]{:S(2)}) collective-permute-start(bf16[192,384]{1,0:T(8,128)(2,1)S(1)} %get-tuple-element.17), channel_id=1, source_target_pairs={{0,32},{4,36},{8,40},{12,44},{16,48},{20,52},{24,56},{28,60},{32,6... | collective-permute-start | bytes 442376 | tf_op jit(solution)/shard_map/ppermute | solution.py:20
  187.1 18.9 %collective-permute-start.23 = (bf16[192,384]{1,0:T(8,128)(2,1)S(1)}, bf16[192,384]{1,0:T(8,128)(2,1)S(1)}, u32[]{:S(2)}, u32[]{:S(2)}) collective-permute-start(bf16[192,384]{1,0:T(8,128)(2,1)S(1)} %get-tuple-element.16), channel_id=1, source_target_pairs={{0,36},{4,40},{8,44},{12,48},{16,52},{20,56},{24,60},{28,64},{32,6... | collective-permute-start | bytes 442376 | tf_op jit(solution)/shard_map/ppermute | solution.py:20
Sparse Core Ops, SparseCore 0:
  23.3 31.7 all-gather.1
where the time goes:
time: 215 us; the launch traced here: 214 us
  starting transfers between devices  148 us (69%)
  waiting for transfers between devices  29.6 us (14%)
  between operations  14.9 us (7%)
  matrix products  9.64 us (4%)
  local copies, waits for them, and re-layouts  6.41 us (3%)
  other arithmetic  5.48 us (3%)
    ppermute x32, starting transfers between devices, shifted(): lax.ppermute(value, axis, [(source, source + steps) for source in range(f...  148 us
    ppermute x32, waiting for transfers between devices, shifted(): lax.ppermute(value, axis, [(source, source + steps) for source in range(f...  29.6 us
    dot_general x7, matrix products, contract_last(): lax.dot_general(left_matrix, right_matrix, (((1,), (1,)), ((), ())), pref...  4.67 us
    unnamed x38, local copies, waits for them, and re-layouts  4.48 us
  transfers between devices with their start and end apart: 33, of which 6 were waited for; matrix products, arithmetic and copies ran while one was open for 6% of the time, Pallas kernels for 0%

commit v1 on v0

v1 whole, which is shorter than its diff:
```python
import functools
import math

import jax
import jax.numpy as jnp
from jax import lax
from jax.experimental import pallas as pl
from jax.experimental.pallas import tpu as pltpu
from jax.sharding import PartitionSpec as P

MESH = pl.DeviceIdType.MESH
HEAD_DIM = 128
F1, F2, F3, F4, F5, F6A, F6B, F7 = range(8)
R1, R2, R3, R4, R5, R6A, R6B, R7 = range(8, 16)
STEPS = 16
F32 = jnp.float32
BF16 = jnp.bfloat16


def dot_nt(a, b):
    return lax.dot_general(a, b, (((1,), (1,)), ((), ())), preferred_element_type=F32)


def dot_nn(a, b):
    return lax.dot_general(a, b, (((1,), (0,)), ((), ())), preferred_element_type=F32)


def dot_tn(a, b):
    return lax.dot_general(a, b, (((0,), (0,)), ((), ())), preferred_element_type=F32)


def kernel(
    heads, rows, nz, ny, nx,
    q_hbm, k_hbm, v_hbm, nb_hbm, w_hbm, g_hbm,
    o_hbm, dq_hbm, dk_hbm, dv_hbm,
    nb, q, kv, w, g, grad, grad_t, scores, probs, stats, out_t, part, send, recv, outs,
    load_sem, store_sem, send_sem, recv_sem, x_send, x_recv,
):
    position = lax.axis_index("tok")
    x = lax.axis_index("head")
    core = lax.rem(position, 2)
    y = lax.rem(position // 2, ny)
    z = position // (2 * ny)
    y_half = y // (ny // 2)
    side = 2 * core - 1
    other = 1 - core
    dz = 1 - 2 * y_half

    def tok_at(z_, y_, core_):
        return (lax.rem(z_ + nz, nz) * ny + lax.rem(y_ + ny, ny)) * 2 + core_

    partner = (tok_at(z, y, other), x)
    outer = (tok_at(z, y + side, other), x)
    far = (tok_at(z, y + ny // 2 + side, other), x)
    z_next = (tok_at(z + dz, y, core), x)
    z_prev = (tok_at(z - dz, y, core), x)
    x_right = (position, lax.rem(x + 1, nx))
    x_left = (position, lax.rem(x + nx - 1, nx))
    peers = [partner, outer, far, z_next, z_prev, x_right, x_left]

    d_model = w.shape[1]
    half = d_model // 2
    scale = 1.0 / math.sqrt(HEAD_DIM)
    scale2 = scale * math.log2(math.e)

    def load(src, dst, index):
        return pltpu.make_async_copy(src, dst, load_sem.at[index])

    def columns(h):
        return pl.ds(h * HEAD_DIM, HEAD_DIM)

    own = pl.ds(0, rows)

    def tile(i):
        return pl.ds(i * rows, rows)

    x_rows = pl.multiple_of(x * (rows // nx), rows // nx)
    my_rows = pl.ds(x_rows, rows // nx)
    loads = {}
    for h in range(heads):
        loads["k", h] = load(k_hbm.at[:, columns(h)], kv.at[h, 0, 0, own], 3 * h)
        loads["v", h] = load(v_hbm.at[:, columns(h)], kv.at[h, 0, 1, own], 3 * h + 1)
        loads["q", h] = load(q_hbm.at[:, columns(h)], q.at[h], 3 * h + 2)
    loads["g"] = load(g_hbm, g.at[my_rows], 3 * heads)
    loads["nb"] = load(nb_hbm, nb, 3 * heads + 1)
    loads["w"] = load(w_hbm, w, 3 * heads + 2)
    for h in range(heads):
        loads["k", h].start()
        loads["v", h].start()
    loads["g"].start()
    for h in range(heads):
        loads["q", h].start()
    loads["nb"].start()
    loads["w"].start()

    barrier = pltpu.get_barrier_semaphore()
    for peer in peers:
        pl.semaphore_signal(barrier, inc=1, device_id=peer, device_id_type=MESH)
    pl.semaphore_wait(barrier, len(peers))

    def remote(h, step, src, dst, device):
        return pltpu.make_async_remote_copy(
            src_ref=src, dst_ref=dst, send_sem=send_sem.at[h, step], recv_sem=recv_sem.at[h, step],
            device_id=device, device_id_type=MESH,
        )

    def keys_of(h, group, index):
        return kv.at[h, group, :, tile(index)]

    copies = {}
    for h in range(heads):
        copies[h, F1] = remote(h, F1, keys_of(h, 0, 0), keys_of(h, 0, 1), partner)
        copies[h, F2] = remote(h, F2, keys_of(h, 0, 0), keys_of(h, 0, 2), outer)
        copies[h, F3] = remote(h, F3, keys_of(h, 0, 0), keys_of(h, 1, 0), far)
        copies[h, F4] = remote(h, F4, keys_of(h, 1, 0), keys_of(h, 1, 1), outer)
        copies[h, F5] = remote(h, F5, keys_of(h, 1, 1), keys_of(h, 1, 2), partner)
        copies[h, F6A] = remote(h, F6A, keys_of(h, 1, 0), keys_of(h, 2, 0), z_next)
        copies[h, F6B] = remote(h, F6B, keys_of(h, 1, 1), keys_of(h, 2, 1), z_next)
        copies[h, F7] = remote(h, F7, keys_of(h, 2, 1), keys_of(h, 2, 2), partner)
        back = {R1: partner, R2: outer, R3: far, R4: outer, R5: partner, R6A: z_prev, R6B: z_prev, R7: partner}
        for step, device in back.items():
            copies[h, step] = remote(h, step, send.at[h, step - R1], recv.at[h, step - R1], device)

    def start(h, *steps):
        for step in steps:
            copies[h, step].start()

    def arrive(h, *steps):
        for step in steps:
            copies[h, step].wait_recv()

    def x_copy(index, row_block, column_block, device):
        block = g.at[pl.ds(row_block, rows // nx), pl.ds(column_block * half, half)]
        return pltpu.make_async_remote_copy(
            src_ref=block, dst_ref=block, send_sem=x_send.at[index], recv_sem=x_recv.at[index],
            device_id=device, device_id_type=MESH,
        )

    left_rows = pl.multiple_of(lax.rem(x + nx - 1, nx) * (rows // nx), rows // nx)
    right_rows = pl.multiple_of(lax.rem(x + 1, nx) * (rows // nx), rows // nx)
    x_copies = [
        x_copy(0, x_rows, 0, x_right),
        x_copy(1, x_rows, 1, x_left),
        x_copy(2, x_rows, 1, x_right),
        x_copy(3, x_rows, 0, x_left),
        x_copy(4, left_rows, 0, x_right),
        x_copy(5, right_rows, 1, x_left),
    ]

    toward = 1 - 2 * y_half
    row_offset = (0, toward, -toward)

    def entries(group):
        base = 9 + (row_offset[group] + 1) * 3 + 1
        if group == 0:
            return (base, base - side, base + side)
        return (base + side, base, base - side)

    def relay1(h):
        arrive(h, F3)
        start(h, F4, F6A)

    def relay2(h):
        arrive(h, F4)
        start(h, F5, F6B)

    def relay3(h):
        arrive(h, F6B)
        start(h, F7)

    def x_relay():
        x_copies[0].wait_recv()
        x_copies[4].start()
        x_copies[1].wait_recv()
        x_copies[5].start()

    def forward(h, group):
        if group == 0:
            loads["q", h].wait()
            arrive(h, F1, F2)
        elif group == 1:
            arrive(h, F5)
        else:
            arrive(h, F6A, F7)
        query = q[h]
        top = jnp.full((1, rows), -1e30, F32)
        for i, entry in enumerate(entries(group)):
            bias = jnp.where(nb[position, entry] >= 0, 0.0, -jnp.inf).astype(F32)
            s = dot_nt(kv[h, group, 0, tile(i)], query) * scale2 + bias
            scores[tile(i)] = s
            top = jnp.maximum(top, jnp.max(s, axis=0, keepdims=True))
        total = jnp.zeros((1, rows), F32)
        attended = jnp.zeros((HEAD_DIM, rows), F32)
        for i in range(3):
            p = jnp.exp2(scores[tile(i)] - top)
            total = total + jnp.sum(p, axis=0, keepdims=True)
            p = p.astype(BF16)
            probs[h, group, tile(i)] = p
            attended = attended + dot_tn(kv[h, group, 1, tile(i)], p)
        stats[h, group, 0:1] = top
        stats[h, group, 1:2] = total
        out_t[h, group] = attended

    def project():
        loads["w"].wait()
        for index in range(2, 6):
            x_copies[index].wait_recv()
        whole = g[...]
        for h in range(heads):
            gt = dot_nt(w[pl.ds(h * HEAD_DIM, HEAD_DIM)], whole)
            grad_t[h] = gt.astype(BF16)
            grad[h] = gt.T.astype(BF16)

    def combine(h):
        tops = [stats[h, group, 0:1] for group in range(3)]
        top = jnp.maximum(jnp.maximum(tops[0], tops[1]), tops[2])
        factors = [jnp.exp2(t - top) for t in tops]
        total = sum(f * stats[h, group, 1:2] for group, f in enumerate(factors))
        attended = jnp.zeros((HEAD_DIM, rows), F32)
        for group in range(3):
            factor = factors[group] / total
            stats[h, group, 2:3] = factor
            attended = attended + out_t[h, group] * factor
        attended = attended.astype(BF16).astype(F32)
        stats[h, 0, 3:4] = jnp.sum(attended * grad_t[h].astype(F32), axis=0, keepdims=True)
        outs[0, h] = attended.T.astype(BF16)
        pltpu.make_async_copy(outs.at[0, h], o_hbm.at[:, columns(h)], store_sem.at[0, h]).start()

    def backward(h, group, emit):
        factor = stats[h, group, 2:3]
        delta = stats[h, 0, 3:4]
        query = q[h]
        grad_rows = grad[h]
        grad_cols = grad_t[h]
        query_t = jnp.zeros((HEAD_DIM, rows), F32)
        for i in range(3):
            weights = (probs[h, group, tile(i)].astype(F32) * factor).astype(BF16)
            dprobs = dot_nn(kv[h, group, 1, tile(i)], grad_cols)
            dscores = (weights.astype(F32) * ((dprobs - delta) * scale)).astype(BF16)
            query_t = query_t + dot_tn(kv[h, group, 0, tile(i)], dscores)
            emit(i, dot_nn(dscores, query), dot_nn(weights, grad_rows))
        if group == 2:
            out_t[h, 0] = query_t
        elif group == 1:
            out_t[h, 0] += query_t
        else:
            outs[1, h] = (out_t[h, 0] + query_t).T.astype(BF16)
            pltpu.make_async_copy(outs.at[1, h], dq_hbm.at[:, columns(h)], store_sem.at[1, h]).start()

    def put(h, step, dk, dv):
        send[h, step - R1, 0] = dk.astype(BF16)
        send[h, step - R1, 1] = dv.astype(BF16)
        start(h, step)

    def keep(h, slot, dk, dv):
        part[h, slot, 0] = dk
        part[h, slot, 1] = dv

    def emit_side(h):
        def emit(i, dk, dv):
            if i == 0:
                put(h, R6A, dk, dv)
            elif i == 1:
                keep(h, 0, dk, dv)
            else:
                put(h, R7, dk, dv)
        return emit

    def emit_far(h):
        def emit(i, dk, dv):
            if i == 0:
                keep(h, 1, dk, dv)
            elif i == 1:
                keep(h, 2, dk, dv)
            else:
                put(h, R5, dk, dv)
        return emit

    def emit_own(h):
        def emit(i, dk, dv):
            if i == 0:
                keep(h, 3, dk, dv)
            elif i == 1:
                put(h, R1, dk, dv)
            else:
                put(h, R2, dk, dv)
        return emit

    def gather_sum(h, slot, step, *steps):
        arrive(h, *steps)
        for i in range(2):
            total = part[h, slot, i]
            for other_step in steps:
                total = total + recv[h, other_step - R1, i].astype(F32)
            send[h, step - R1, i] = total.astype(BF16)
        start(h, step)

    def back2(h):
        backward(h, 2, emit_side(h))

    def back1(h):
        backward(h, 1, emit_far(h))

    def back0(h):
        backward(h, 0, emit_own(h))

    def sum_side(h):
        gather_sum(h, 0, R6B, R7)

    def sum_far(h):
        gather_sum(h, 2, R4, R5, R6B)

    def sum_outer(h):
        gather_sum(h, 1, R3, R6A, R4)

    def finish(h):
        arrive(h, R1, R2, R3)
        for i, out in enumerate((dk_hbm, dv_hbm)):
            total = part[h, 3, i]
            for step in (R1, R2, R3):
                total = total + recv[h, step - R1, i].astype(F32)
            outs[2 + i, h] = total.astype(BF16)
            pltpu.make_async_copy(outs.at[2 + i, h], out.at[:, columns(h)], store_sem.at[2 + i, h]).start()

    for h in range(heads):
        loads["k", h].wait()
        loads["v", h].wait()
        start(h, F3, F2, F1)
    loads["g"].wait()
    for index in range(4):
        x_copies[index].start()
    loads["nb"].wait()

    relay1(0)
    forward(0, 0)
    x_relay()
    relay2(0)
    relay1(1)
    forward(1, 0)
    relay2(1)
    forward(0, 1)
    relay1(2)
    relay3(0)
    forward(2, 0)
    relay2(2)
    forward(1, 1)
    relay3(1)
    forward(0, 2)
    project()
    combine(0)
    back2(0)
    relay3(2)
    forward(2, 1)
    forward(1, 2)
    sum_side(0)
    back1(0)
    combine(1)
    back2(1)
    sum_far(0)
    forward(2, 2)
    back0(0)
    sum_side(1)
    sum_outer(0)
    back1(1)
    combine(2)
    back2(2)
    sum_far(1)
    back0(1)
    sum_side(2)
    back1(2)
    sum_outer(1)
    finish(0)
    sum_far(2)
    back0(2)
    finish(1)
    sum_outer(2)
    finish(2)

    for h in range(heads):
        for step in range(STEPS):
            copies[h, step].wait_send()
        for i, out in enumerate((o_hbm, dq_hbm, dk_hbm, dv_hbm)):
            pltpu.make_async_copy(outs.at[i, h], out.at[:, columns(h)], store_sem.at[i, h]).wait()
    for copy in x_copies:
        copy.wait_send()


def local(nz, ny, nx, query_rows, key_rows, value_rows, neighbours, out_weight, out_grad):
    rows, width = query_rows.shape
    heads = width // HEAD_DIM
    d_model = out_weight.shape[1]
    any_spec = pl.BlockSpec(memory_space=pl.ANY)
    return pl.pallas_call(
        functools.partial(kernel, heads, rows, nz, ny, nx),
        out_shape=[jax.ShapeDtypeStruct((rows, width), BF16)] * 4,
        in_specs=[any_spec] * 6,
        out_specs=[any_spec] * 4,
        scratch_shapes=[
            pltpu.SMEM(neighbours.shape, jnp.int32),
            pltpu.VMEM((heads, rows, HEAD_DIM), BF16),
            pltpu.VMEM((heads, 3, 2, 3 * rows, HEAD_DIM), BF16),
            pltpu.VMEM((width, d_model), BF16),
            pltpu.VMEM((rows, d_model), BF16),
            pltpu.VMEM((heads, rows, HEAD_DIM), BF16),
            pltpu.VMEM((heads, HEAD_DIM, rows), BF16),
            pltpu.VMEM((3 * rows, rows), F32),
            pltpu.VMEM((heads, 3, 3 * rows, rows), BF16),
            pltpu.VMEM((heads, 3, 8, rows), F32),
            pltpu.VMEM((heads, 3, HEAD_DIM, rows), F32),
            pltpu.VMEM((heads, 4, 2, rows, HEAD_DIM), F32),
            pltpu.VMEM((heads, 8, 2, rows, HEAD_DIM), BF16),
            pltpu.VMEM((heads, 8, 2, rows, HEAD_DIM), BF16),
            pltpu.VMEM((4, heads, rows, HEAD_DIM), BF16),
            pltpu.SemaphoreType.DMA((3 * heads + 3,)),
            pltpu.SemaphoreType.DMA((4, heads)),
            pltpu.SemaphoreType.DMA((heads, STEPS)),
            pltpu.SemaphoreType.DMA((heads, STEPS)),
            pltpu.SemaphoreType.DMA((6,)),
            pltpu.SemaphoreType.DMA((6,)),
        ],
        compiler_params=pltpu.CompilerParams(
            collective_id=0, has_side_effects=True, vmem_limit_bytes=48 * 1024 * 1024
        ),
    )(query_rows, key_rows, value_rows, neighbours, out_weight, out_grad)


def solution(mesh):
    nx = mesh.shape["head"]
    ny = 8
    nz = mesh.shape["tok"] // (2 * ny)
    in_specs = (
        P("tok", "head"),
        P("tok", "head"),
        P("tok", "head"),
        P(),
        P("head", None),
        P(("tok", "head"), None),
    )
    out_specs = (P("tok", "head"), P("tok", "head"), P("tok", "head"), P("tok", "head"))
    return jax.shard_map(
        functools.partial(local, nz, ny, nx), mesh=mesh, in_specs=in_specs, out_specs=out_specs, check_vma=False
    )
```

time: 215 us -> 82.1 us (0.38)
  the two profiles are of different devices: /device:TPU:458 before, /device:TPU:1 now
where the time goes in v1:
time: 82.1 us; the launch traced here: 81.8 us
  Pallas kernels  72.3 us (88%)
  local copies, waits for them, and re-layouts  8.81 us (11%)
    pallas_call x1, Pallas kernels, local(): pl.pallas_call(functools.partial(kernel, heads, rows, nz, ny, nx), out_sh...  72.3 us
    unnamed x15, local copies, waits for them, and re-layouts  8.81 us

profile of v1, /device:TPU:1, one launch (start us, length us, event | category | flops | bytes accessed | tf_op | source)
XLA Modules:
  0.0 81.8 jit_solution(8469828326072986421)
XLA Ops:
  0.6 0.8 %copy.10.nb_hbm = s32[128,27]{1,0:T(8,128)S(1)} copy(s32[128,27]{0,1:T(8,128)} %param.9) | data formatting | bytes 27648 | tf_op args[3]
  1.4 0.0 copy-start
  1.5 1.7 %copy-done = bf16[384,3072]{1,0:T(8,128)(2,1)S(1)} copy-done((bf16[384,3072]{1,0:T(8,128)(2,1)S(1)}, bf16[384,3072]{1,0:T(8,128)(2,1)}, u32[]{:S(2)}) %copy-start) | copy-done | bytes 2359320
  3.1 0.0 copy-start.1
  3.1 1.0 %copy-done.1 = bf16[48,3072]{1,0:T(8,128)(2,1)S(1)} copy-done((bf16[48,3072]{1,0:T(8,128)(2,1)S(1)}, bf16[48,3072]{1,0:T(8,128)(2,1)}, u32[]{:S(2)}) %copy-start.1) | copy-done | bytes 294936
  4.1 0.0 copy-start.2
  4.1 0.9 %copy-done.2 = bf16[192,384]{1,0:T(8,128)(2,1)S(1)} copy-done((bf16[192,384]{1,0:T(8,128)(2,1)S(1)}, bf16[192,384]{1,0:T(8,128)(2,1)}, u32[]{:S(2)}) %copy-start.2) | copy-done | bytes 147480
  5.0 0.0 copy-start.3
  5.0 0.9 %copy-done.3 = bf16[192,384]{1,0:T(8,128)(2,1)S(1)} copy-done((bf16[192,384]{1,0:T(8,128)(2,1)S(1)}, bf16[192,384]{1,0:T(8,128)(2,1)}, u32[]{:S(2)}) %copy-start.3) | copy-done | bytes 147480
  5.9 0.0 copy-start.4
  5.9 0.9 %copy-done.4 = bf16[192,384]{1,0:T(8,128)(2,1)S(1)} copy-done((bf16[192,384]{1,0:T(8,128)(2,1)S(1)}, bf16[192,384]{1,0:T(8,128)(2,1)}, u32[]{:S(2)}) %copy-start.4) | copy-done | bytes 147480
  6.8 72.3 %shard_map.93 = (bf16[192,384]{1,0:T(8,128)(2,1)S(1)}, bf16[192,384]{1,0:T(8,128)(2,1)S(1)}, bf16[192,384]{1,0:T(8,128)(2,1)S(1)}, bf16[192,384]{1,0:T(8,128)(2,1)S(1)}) custom-call(bf16[192,384]{1,0:T(8,128)(2,1)S(1)} %copy-done.2, bf16[192,384]{1,0:T(8,128)(2,1)S(1)} %copy-done.3, bf16[192,384]{1,0:T(8,128)(2,1)S(1)} %copy-done.4, ...), custom_call_target="tpu_custom_call" | custom-call | tf_op jit(solution)/shard_map/pallas_call | solution.py:393
  79.1 0.7 copy.15
  79.8 0.7 copy.16
  80.4 0.7 copy.17
  81.1 0.7 copy.18
Async XLA Ops:
  1.4 1.7 %copy-start = (bf16[384,3072]{1,0:T(8,128)(2,1)S(1)}, bf16[384,3072]{1,0:T(8,128)(2,1)}, u32[]{:S(2)}) copy-start(bf16[384,3072]{1,0:T(8,128)(2,1)} %w_hbm.1) | copy-start | bytes 7077892
  3.1 1.0 %copy-start.1 = (bf16[48,3072]{1,0:T(8,128)(2,1)S(1)}, bf16[48,3072]{1,0:T(8,128)(2,1)}, u32[]{:S(2)}) copy-start(bf16[48,3072]{1,0:T(8,128)(2,1)} %g_hbm.1) | copy-start | bytes 884740
  4.1 0.9 %copy-start.2 = (bf16[192,384]{1,0:T(8,128)(2,1)S(1)}, bf16[192,384]{1,0:T(8,128)(2,1)}, u32[]{:S(2)}) copy-start(bf16[192,384]{1,0:T(8,128)(2,1)} %q_hbm.1) | copy-start | bytes 442372
  5.0 0.9 %copy-start.3 = (bf16[192,384]{1,0:T(8,128)(2,1)S(1)}, bf16[192,384]{1,0:T(8,128)(2,1)}, u32[]{:S(2)}) copy-start(bf16[192,384]{1,0:T(8,128)(2,1)} %k_hbm.1) | copy-start | bytes 442372
  5.9 0.9 %copy-start.4 = (bf16[192,384]{1,0:T(8,128)(2,1)S(1)}, bf16[192,384]{1,0:T(8,128)(2,1)}, u32[]{:S(2)}) copy-start(bf16[192,384]{1,0:T(8,128)(2,1)} %v_hbm.1) | copy-start | bytes 442372

commit v2 on v1

--- a/solution.py
+++ b/solution.py
@@ -32,7 +32,7 @@
 def kernel(
     heads, rows, nz, ny, nx,
     q_hbm, k_hbm, v_hbm, nb_hbm, w_hbm, g_hbm,
-    o_hbm, dq_hbm, dk_hbm, dv_hbm,
+    packed,
     nb, q, kv, w, g, grad, grad_t, scores, probs, stats, out_t, part, send, recv, outs,
     load_sem, store_sem, send_sem, recv_sem, x_send, x_recv,
 ):
@@ -66,6 +66,9 @@
     def load(src, dst, index):
         return pltpu.make_async_copy(src, dst, load_sem.at[index])
 
+    def store(i, h):
+        return pltpu.make_async_copy(outs.at[i, h], packed.at[i, h], store_sem.at[i, h])
+
     def columns(h):
         return pl.ds(h * HEAD_DIM, HEAD_DIM)
 
@@ -158,7 +161,7 @@
 
     def relay1(h):
         arrive(h, F3)
-        start(h, F4, F6A)
+        start(h, F4, F6A, F2)
 
     def relay2(h):
         arrive(h, F4)
@@ -176,7 +179,6 @@
 
     def forward(h, group):
         if group == 0:
-            loads["q", h].wait()
             arrive(h, F1, F2)
         elif group == 1:
             arrive(h, F5)
@@ -185,7 +187,7 @@
         query = q[h]
         top = jnp.full((1, rows), -1e30, F32)
         for i, entry in enumerate(entries(group)):
-            bias = jnp.where(nb[position, entry] >= 0, 0.0, -jnp.inf).astype(F32)
+            bias = jnp.where(nb[entry, position] >= 0, 0.0, -jnp.inf).astype(F32)
             s = dot_nt(kv[h, group, 0, tile(i)], query) * scale2 + bias
             scores[tile(i)] = s
             top = jnp.maximum(top, jnp.max(s, axis=0, keepdims=True))
@@ -224,7 +226,7 @@
         attended = attended.astype(BF16).astype(F32)
         stats[h, 0, 3:4] = jnp.sum(attended * grad_t[h].astype(F32), axis=0, keepdims=True)
         outs[0, h] = attended.T.astype(BF16)
-        pltpu.make_async_copy(outs.at[0, h], o_hbm.at[:, columns(h)], store_sem.at[0, h]).start()
+        store(0, h).start()
 
     def backward(h, group, emit):
         factor = stats[h, group, 2:3]
@@ -245,7 +247,7 @@
             out_t[h, 0] += query_t
         else:
             outs[1, h] = (out_t[h, 0] + query_t).T.astype(BF16)
-            pltpu.make_async_copy(outs.at[1, h], dq_hbm.at[:, columns(h)], store_sem.at[1, h]).start()
+            store(1, h).start()
 
     def put(h, step, dk, dv):
         send[h, step - R1, 0] = dk.astype(BF16)
@@ -315,88 +317,108 @@
 
     def finish(h):
         arrive(h, R1, R2, R3)
-        for i, out in enumerate((dk_hbm, dv_hbm)):
+        for i in range(2):
             total = part[h, 3, i]
             for step in (R1, R2, R3):
                 total = total + recv[h, step - R1, i].astype(F32)
             outs[2 + i, h] = total.astype(BF16)
-            pltpu.make_async_copy(outs.at[2 + i, h], out.at[:, columns(h)], store_sem.at[2 + i, h]).start()
+            store(2 + i, h).start()
 
     for h in range(heads):
         loads["k", h].wait()
         loads["v", h].wait()
-        start(h, F3, F2, F1)
+        start(h, F3, F1)
     loads["g"].wait()
     for index in range(4):
         x_copies[index].start()
     loads["nb"].wait()
+    for h in range(heads):
+        loads["q", h].wait()
 
     relay1(0)
-    forward(0, 0)
     x_relay()
     relay2(0)
+    forward(0, 1)
     relay1(1)
-    forward(1, 0)
+    forward(0, 0)
+    relay3(0)
+    project()
+    forward(0, 2)
     relay2(1)
-    forward(0, 1)
-    relay1(2)
-    relay3(0)
-    forward(2, 0)
-    relay2(2)
-    forward(1, 1)
-    relay3(1)
-    forward(0, 2)
-    project()
     combine(0)
     back2(0)
-    relay3(2)
-    forward(2, 1)
+    forward(1, 1)
+    sum_side(0)
+    relay1(2)
+    back1(0)
+    relay3(1)
+    forward(1, 0)
+    back0(0)
+    relay2(2)
     forward(1, 2)
-    sum_side(0)
-    back1(0)
     combine(1)
     back2(1)
+    forward(2, 1)
+    sum_side(1)
+    relay3(2)
+    back1(1)
     sum_far(0)
+    forward(2, 0)
     forward(2, 2)
-    back0(0)
-    sum_side(1)
-    sum_outer(0)
-    back1(1)
     combine(2)
     back2(2)
-    sum_far(1)
     back0(1)
     sum_side(2)
+    sum_outer(0)
     back1(2)
+    sum_far(1)
+    back0(2)
     sum_outer(1)
+    sum_far(2)
     finish(0)
-    sum_far(2)
-    back0(2)
+    sum_outer(2)
     finish(1)
-    sum_outer(2)
     finish(2)
 
     for h in range(heads):
         for step in range(STEPS):
             copies[h, step].wait_send()
-        for i, out in enumerate((o_hbm, dq_hbm, dk_hbm, dv_hbm)):
-            pltpu.make_async_copy(outs.at[i, h], out.at[:, columns(h)], store_sem.at[i, h]).wait()
+        for i in range(4):
+            store(i, h).wait()
     for copy in x_copies:
         copy.wait_send()
+
+
+def unpack(heads, packed, *refs):
+    results, scratch, in_sem, out_sem = refs[:4], refs[4], refs[5], refs[6]
+    loads = []
+    for i in range(4):
+        for h in range(heads):
+            block = scratch.at[i, :, pl.ds(h * HEAD_DIM, HEAD_DIM)]
+            loads.append(pltpu.make_async_copy(packed.at[i, h], block, in_sem.at[i, h]))
+    for copy in loads:
+        copy.start()
+    stores = [pltpu.make_async_copy(scratch.at[i], result, out_sem.at[i]) for i, result in enumerate(results)]
+    for i in range(4):
+        for h in range(heads):
+            loads[i * heads + h].wait()
+        stores[i].start()
+    for copy in stores:
+        copy.wait()
 
 
 def local(nz, ny, nx, query_rows, key_rows, value_rows, neighbours, out_weight, out_grad):
     rows, width = query_rows.shape
     heads = width // HEAD_DIM
     d_model = out_weight.shape[1]
-    any_spec = pl.BlockSpec(memory_space=pl.ANY)
-    return pl.pallas_call(
+    hbm = pl.BlockSpec(memory_space=pltpu.HBM)
+    packed = pl.pallas_call(
         functools.partial(kernel, heads, rows, nz, ny, nx),
-        out_shape=[jax.ShapeDtypeStruct((rows, width), BF16)] * 4,
-        in_specs=[any_spec] * 6,
-        out_specs=[any_spec] * 4,
+        out_shape=jax.ShapeDtypeStruct((4, heads, rows, HEAD_DIM), BF16),
+        in_specs=[hbm] * 6,
+        out_specs=hbm,
         scratch_shapes=[
-            pltpu.SMEM(neighbours.shape, jnp.int32),
+            pltpu.SMEM(neighbours.shape[::-1], jnp.int32),
             pltpu.VMEM((heads, rows, HEAD_DIM), BF16),
             pltpu.VMEM((heads, 3, 2, 3 * rows, HEAD_DIM), BF16),
             pltpu.VMEM((width, d_model), BF16),
@@ -419,9 +441,20 @@
             pltpu.SemaphoreType.DMA((6,)),
         ],
         compiler_params=pltpu.CompilerParams(
-            collective_id=0, has_side_effects=True, vmem_limit_bytes=48 * 1024 * 1024
+            collective_id=0, has_side_effects=True, vmem_limit_bytes=63 * 1024 * 1024
         ),
-    )(query_rows, key_rows, value_rows, neighbours, out_weight, out_grad)
+    )(query_rows, key_rows, value_rows, neighbours.T, out_weight, out_grad)
+    return pl.pallas_call(
+        functools.partial(unpack, heads),
+        out_shape=[jax.ShapeDtypeStruct((rows, width), BF16)] * 4,
+        in_specs=[hbm],
+        out_specs=[hbm] * 4,
+        scratch_shapes=[
+            pltpu.VMEM((4, rows, width), BF16),
+            pltpu.SemaphoreType.DMA((4, heads)),
+            pltpu.SemaphoreType.DMA((4,)),
+        ],
+    )(packed)
 
 
 def solution(mesh):

time: 82.1 us -> 66.8 us (0.81)
  the two profiles are of different devices: /device:TPU:1 before, /device:TPU:2 now
where the time goes in v2:
time: 66.8 us; the launch traced here: 66.6 us
  Pallas kernels  65.9 us (99%)
    pallas_call x1, Pallas kernels, local(): pl.pallas_call(functools.partial(kernel, heads, rows, nz, ny, nx), out_sh...  64.1 us
    pallas_call x1, Pallas kernels, local(): pl.pallas_call(functools.partial(unpack, heads), out_shape=[jax.ShapeDtyp...  1.86 us

profile of v2, /device:TPU:2, one launch (start us, length us, event | category | flops | bytes accessed | tf_op | source)
XLA Modules:
  0.0 66.6 jit_solution(8705206445679961767)
XLA Ops:
  0.6 64.1 %shard_map.93.packed = bf16[4,3,192,128]{3,2,1,0:T(8,128)(2,1)} custom-call(bf16[192,384]{1,0:T(8,128)(2,1)} %q_hbm.1, bf16[192,384]{1,0:T(8,128)(2,1)} %k_hbm.1, bf16[192,384]{1,0:T(8,128)(2,1)} %v_hbm.1, s32[27,128]{1,0:T(8,128)} %bitcast.1, bf16[384,3072]{1,0:T(8,128)(2,1)} %w_hbm.1, bf16[48,3072]{1,0:T(8,128)(2,1)} %g_hbm.1), custom_call_target="tpu_custom_call" | custom-call | tf_op jit(solution)/shard_map/pallas_call | solution.py:415
  64.7 1.9 %shard_map.94 = (bf16[192,384]{1,0:T(8,128)(2,1)}, bf16[192,384]{1,0:T(8,128)(2,1)}, bf16[192,384]{1,0:T(8,128)(2,1)}, bf16[192,384]{1,0:T(8,128)(2,1)}) custom-call(bf16[4,3,192,128]{3,2,1,0:T(8,128)(2,1)} %shard_map.93.packed), custom_call_target="tpu_custom_call" | custom-call | tf_op jit(solution)/shard_map/pallas_call | solution.py:447

commit v3 on v2

--- a/solution.py
+++ b/solution.py
@@ -13,6 +13,7 @@
 F1, F2, F3, F4, F5, F6A, F6B, F7 = range(8)
 R1, R2, R3, R4, R5, R6A, R6B, R7 = range(8, 16)
 STEPS = 16
+SPLIT = (R3, R4, R6B, R7)
 F32 = jnp.float32
 BF16 = jnp.bfloat16
 
@@ -101,9 +102,9 @@
         pl.semaphore_signal(barrier, inc=1, device_id=peer, device_id_type=MESH)
     pl.semaphore_wait(barrier, len(peers))
 
-    def remote(h, step, src, dst, device):
+    def remote(h, step, src, dst, device, half=0):
         return pltpu.make_async_remote_copy(
-            src_ref=src, dst_ref=dst, send_sem=send_sem.at[h, step], recv_sem=recv_sem.at[h, step],
+            src_ref=src, dst_ref=dst, send_sem=send_sem.at[h, step, half], recv_sem=recv_sem.at[h, step, half],
             device_id=device, device_id_type=MESH,
         )
 
@@ -122,7 +123,12 @@
         copies[h, F7] = remote(h, F7, keys_of(h, 2, 1), keys_of(h, 2, 2), partner)
         back = {R1: partner, R2: outer, R3: far, R4: outer, R5: partner, R6A: z_prev, R6B: z_prev, R7: partner}
         for step, device in back.items():
-            copies[h, step] = remote(h, step, send.at[h, step - R1], recv.at[h, step - R1], device)
+            here, there = send.at[h, step - R1], recv.at[h, step - R1]
+            if step in SPLIT:
+                for i in range(2):
+                    copies[h, step, i] = remote(h, step, here.at[i], there.at[i], device, i)
+            else:
+                copies[h, step] = remote(h, step, here, there, device)
 
     def start(h, *steps):
         for step in steps:
@@ -250,9 +256,12 @@
             store(1, h).start()
 
     def put(h, step, dk, dv):
-        send[h, step - R1, 0] = dk.astype(BF16)
-        send[h, step - R1, 1] = dv.astype(BF16)
-        start(h, step)
+        for i, term in enumerate((dk, dv)):
+            send[h, step - R1, i] = term.astype(BF16)
+            if step in SPLIT:
+                copies[h, step, i].start()
+        if step not in SPLIT:
+            start(h, step)
 
     def keep(h, slot, dk, dv):
         part[h, slot, 0] = dk
@@ -289,13 +298,17 @@
         return emit
 
     def gather_sum(h, slot, step, *steps):
-        arrive(h, *steps)
         for i in range(2):
+            for other_step in steps:
+                if other_step in SPLIT:
+                    copies[h, other_step, i].wait_recv()
+                elif i == 0:
+                    arrive(h, other_step)
             total = part[h, slot, i]
             for other_step in steps:
                 total = total + recv[h, other_step - R1, i].astype(F32)
             send[h, step - R1, i] = total.astype(BF16)
-        start(h, step)
+            copies[h, step, i].start()
 
     def back2(h):
         backward(h, 2, emit_side(h))
@@ -316,8 +329,9 @@
         gather_sum(h, 1, R3, R6A, R4)
 
     def finish(h):
-        arrive(h, R1, R2, R3)
+        arrive(h, R1, R2)
         for i in range(2):
+            copies[h, R3, i].wait_recv()
             total = part[h, 3, i]
             for step in (R1, R2, R3):
                 total = total + recv[h, step - R1, i].astype(F32)
@@ -382,7 +396,8 @@
 
     for h in range(heads):
         for step in range(STEPS):
-            copies[h, step].wait_send()
+            for key in ([(h, step, 0), (h, step, 1)] if step in SPLIT else [(h, step)]):
+                copies[key].wait_send()
         for i in range(4):
             store(i, h).wait()
     for copy in x_copies:
@@ -435,8 +450,8 @@
             pltpu.VMEM((4, heads, rows, HEAD_DIM), BF16),
             pltpu.SemaphoreType.DMA((3 * heads + 3,)),
             pltpu.SemaphoreType.DMA((4, heads)),
-            pltpu.SemaphoreType.DMA((heads, STEPS)),
-            pltpu.SemaphoreType.DMA((heads, STEPS)),
+            pltpu.SemaphoreType.DMA((heads, STEPS, 2)),
+            pltpu.SemaphoreType.DMA((heads, STEPS, 2)),
             pltpu.SemaphoreType.DMA((6,)),
             pltpu.SemaphoreType.DMA((6,)),
         ],

time: 66.8 us -> 68.3 us (1.022)
  Pallas kernels: 65.9 us -> 67.2 us
    pallas_call x1, Pallas kernels: 64.1 us -> 65.3 us  [local(): pl.pallas_call(functools.partial(kernel, heads, rows, nz, ny, nx), out_sh...]
where the time goes in v3:
time: 68.3 us; the launch traced here: 67.8 us
  Pallas kernels  67.2 us (98%)
    pallas_call x1, Pallas kernels, local(): pl.pallas_call(functools.partial(kernel, heads, rows, nz, ny, nx), out_sh...  65.3 us
    pallas_call x1, Pallas kernels, local(): pl.pallas_call(functools.partial(unpack, heads), out_shape=[jax.ShapeDtyp...  1.86 us

profile of v3, /device:TPU:2, one launch (start us, length us, event | category | flops | bytes accessed | tf_op | source)
XLA Modules:
  0.0 67.8 jit_solution(12666476397107193354)
XLA Ops:
  0.6 65.3 %shard_map.93.packed = bf16[4,3,192,128]{3,2,1,0:T(8,128)(2,1)} custom-call(bf16[192,384]{1,0:T(8,128)(2,1)} %q_hbm.1, bf16[192,384]{1,0:T(8,128)(2,1)} %k_hbm.1, bf16[192,384]{1,0:T(8,128)(2,1)} %v_hbm.1, s32[27,128]{1,0:T(8,128)} %bitcast.1, bf16[384,3072]{1,0:T(8,128)(2,1)} %w_hbm.1, bf16[48,3072]{1,0:T(8,128)(2,1)} %g_hbm.1), custom_call_target="tpu_custom_call" | custom-call | tf_op jit(solution)/shard_map/pallas_call | solution.py:430
  66.0 1.9 %shard_map.94 = (bf16[192,384]{1,0:T(8,128)(2,1)}, bf16[192,384]{1,0:T(8,128)(2,1)}, bf16[192,384]{1,0:T(8,128)(2,1)}, bf16[192,384]{1,0:T(8,128)(2,1)}) custom-call(bf16[4,3,192,128]{3,2,1,0:T(8,128)(2,1)} %shard_map.93.packed), custom_call_target="tpu_custom_call" | custom-call | tf_op jit(solution)/shard_map/pallas_call | solution.py:462

commit v4 on v2

--- a/solution.py
+++ b/solution.py
@@ -110,9 +110,8 @@
     def keys_of(h, group, index):
         return kv.at[h, group, :, tile(index)]
 
-    copies = {}
-    for h in range(heads):
-        copies[h, F1] = remote(h, F1, keys_of(h, 0, 0), keys_of(h, 0, 1), partner)
+    copies = {(0, F1): remote(0, F1, kv.at[:, 0, :, tile(0)], kv.at[:, 0, :, tile(1)], partner)}
+    for h in range(heads):
         copies[h, F2] = remote(h, F2, keys_of(h, 0, 0), keys_of(h, 0, 2), outer)
         copies[h, F3] = remote(h, F3, keys_of(h, 0, 0), keys_of(h, 1, 0), far)
         copies[h, F4] = remote(h, F4, keys_of(h, 1, 0), keys_of(h, 1, 1), outer)
@@ -179,7 +178,9 @@
 
     def forward(h, group):
         if group == 0:
-            arrive(h, F1, F2)
+            if h == 0:
+                arrive(h, F1)
+            arrive(h, F2)
         elif group == 1:
             arrive(h, F5)
         else:
@@ -327,7 +328,8 @@
     for h in range(heads):
         loads["k", h].wait()
         loads["v", h].wait()
-        start(h, F3, F1)
+        start(h, F3)
+    start(0, F1)
     loads["g"].wait()
     for index in range(4):
         x_copies[index].start()
@@ -382,7 +384,8 @@
 
     for h in range(heads):
         for step in range(STEPS):
-            copies[h, step].wait_send()
+            if (h, step) in copies:
+                copies[h, step].wait_send()
         for i in range(4):
             store(i, h).wait()
     for copy in x_copies:

time: 66.8 us -> 66.8 us (level)
  no operation moved by 1% of the time
where the time goes in v4:
time: 66.8 us; the launch traced here: 66.6 us
  Pallas kernels  65.9 us (99%)
    pallas_call x1, Pallas kernels, local(): pl.pallas_call(functools.partial(kernel, heads, rows, nz, ny, nx), out_sh...  64.1 us
    pallas_call x1, Pallas kernels, local(): pl.pallas_call(functools.partial(unpack, heads), out_shape=[jax.ShapeDtyp...  1.86 us

profile of v4, /device:TPU:2, one launch (start us, length us, event | category | flops | bytes accessed | tf_op | source)
XLA Modules:
  0.0 66.6 jit_solution(9480398476449435616)
XLA Ops:
  0.6 64.1 %shard_map.93.packed = bf16[4,3,192,128]{3,2,1,0:T(8,128)(2,1)} custom-call(bf16[192,384]{1,0:T(8,128)(2,1)} %q_hbm.1, bf16[192,384]{1,0:T(8,128)(2,1)} %k_hbm.1, bf16[192,384]{1,0:T(8,128)(2,1)} %v_hbm.1, s32[27,128]{1,0:T(8,128)} %bitcast.1, bf16[384,3072]{1,0:T(8,128)(2,1)} %w_hbm.1, bf16[48,3072]{1,0:T(8,128)(2,1)} %g_hbm.1), custom_call_target="tpu_custom_call" | custom-call | tf_op jit(solution)/shard_map/pallas_call | solution.py:418
  64.7 1.9 %shard_map.94 = (bf16[192,384]{1,0:T(8,128)(2,1)}, bf16[192,384]{1,0:T(8,128)(2,1)}, bf16[192,384]{1,0:T(8,128)(2,1)}, bf16[192,384]{1,0:T(8,128)(2,1)}) custom-call(bf16[4,3,192,128]{3,2,1,0:T(8,128)(2,1)} %shard_map.93.packed), custom_call_target="tpu_custom_call" | custom-call | tf_op jit(solution)/shard_map/pallas_call | solution.py:450
